TPU v7x, 32 devices: a whole 2x2x4 slice. The times are simulated.
32 devices in a mesh: chan: 4 (over z), row: 4 (over y, core), col: 2 (over x).
Axes of the slice: x: 2, y: 2, z: 4, core: 2. Of those that a mesh axis runs over, the one named last changes fastest.
Arguments:
- voltages: bfloat16 [1024, 262144], P('chan', ('row', 'col')), may hold values from -6 to 6
Outputs:
- visibilities: float32 [256, 2, 1024, 1024], P('chan', None, 'row', 'col')
All inputs are finite; a program needn't handle non-finite values.
Results may differ from a plain program's by a relative error of at most 0.0053.
Values may be sent and summed in bfloat16 or wider, within the bound.
A program may use at most 384 MiB of HBM per device.

v0:
```python
import jax
import jax.numpy as jnp
from jax import lax
from jax.sharding import PartitionSpec as P

FFT_LEN = 512
TAPS = 8
CHANNELS = 256


def shifted(value, axis, by):
    length = lax.axis_size(axis)
    pairs = [(i, i + by) for i in range(length) if 0 <= i + by < length]
    return lax.ppermute(value, axis, pairs)


def window_table(taps, length):
    count = taps * length
    position = jnp.arange(count).astype(jnp.float32)
    offset = (position - count / 2 + 0.5) / length
    taper = 0.5 - 0.5 * jnp.cos(2.0 * jnp.pi * (position + 0.5) / count)
    values = jnp.sinc(offset) * taper
    values = values / jnp.sqrt(jnp.sum(values * values))
    return values.reshape(taps, length)


def fourier_table(channels, length):
    channel_index = jnp.arange(channels, dtype=jnp.int32)[:, None]
    sample_index = jnp.arange(length, dtype=jnp.int32)[None, :]
    phase = (channel_index * sample_index % length).astype(jnp.float32) * (2.0 * jnp.pi / length)
    return jnp.stack([jnp.cos(phase), -jnp.sin(phase)], axis=1).astype(jnp.bfloat16)


def per_device(voltages):
    local_inputs = voltages.shape[0]
    slot_spectra = voltages.shape[1] // FFT_LEN
    window = window_table(TAPS, FFT_LEN)
    table = fourier_table(CHANNELS, FFT_LEN)
    tail = voltages[:, (slot_spectra - TAPS + 1) * FFT_LEN :]
    earlier = shifted(tail, ("row", "col"), 1)
    extended = jnp.concatenate([earlier, voltages], axis=1).reshape(
        local_inputs, slot_spectra + TAPS - 1, FFT_LEN
    )
    total = jnp.zeros((local_inputs, slot_spectra, FFT_LEN), jnp.float32)
    for tap_index in range(TAPS):
        total = total + window[tap_index][None, None, :] * extended[
            :, tap_index : tap_index + slot_spectra, :
        ].astype(jnp.float32)
    filtered = total.astype(jnp.bfloat16)
    spectra = jnp.einsum(
        "kpn,isn->kpsi", table, filtered, preferred_element_type=jnp.float32
    ).astype(jnp.bfloat16)
    turned = lax.all_to_all(spectra, "chan", split_axis=0, concat_axis=3, tiled=True)
    inputs_all = turned.shape[3]
    row_count = lax.axis_size("row")
    col_count = lax.axis_size("col")
    row_block = inputs_all // row_count
    col_block = inputs_all // col_count
    spectra_total = slot_spectra * row_count * col_count
    row_start = lax.axis_index("row") * row_block
    col_start = lax.axis_index("col") * col_block
    piece = lax.all_gather(turned, ("row", "col"), axis=2, tiled=True)
    left = lax.dynamic_slice_in_dim(piece, row_start, row_block, 3)
    right = lax.dynamic_slice_in_dim(piece, col_start, col_block, 3)
    flipped = jnp.stack([left[:, 1], -left[:, 0]], axis=1)
    real_part = jnp.einsum("cpsi,cpsj->cij", left, right, preferred_element_type=jnp.float32)
    imag_part = jnp.einsum("cpsi,cpsj->cij", flipped, right, preferred_element_type=jnp.float32)
    summed = jnp.stack([real_part, imag_part], axis=1)
    return summed / spectra_total


def solution(mesh):
    placed = (P("chan", ("row", "col")),)
    return jax.shard_map(
        per_device,
        mesh=mesh,
        in_specs=placed,
        out_specs=P("chan", None, "row", "col"),
        check_vma=False,
    )
```

profile of v0, /device:TPU:0, one launch (start us, length us, event | category | flops | bytes accessed | tf_op | source)
XLA Modules:
  0.0 1360.3 jit_solution(8309935868669835237)
XLA Ops:
  6.5 0.0 all-gather.2.cloned.1.call-start
  6.5 22.4 %copy.22 = bf16[256,32768]{0,1:T(8,128)(2,1)} copy(bf16[256,32768]{1,0:T(8,128)(2,1)} %param.1) | data formatting | bytes 33554432 | tf_op args[0]
  28.9 1.6 slice.85
  30.5 6.1 collective-permute-start
  36.6 0.7 multiply_reduce_fusion
  38.0 0.1 broadcast_divide_fusion
  38.1 2.2 negate_convert_fusion
  40.3 34.3 %collective-permute-done = bf16[256,3584]{0,1:T(8,128)(2,1)} collective-permute-done((bf16[256,3584]{0,1:T(8,128)(2,1)S(1)}, bf16[256,3584]{0,1:T(8,128)(2,1)}, u32[]{:S(2)}, u32[]{:S(2)}) %collective-permute-start) | collective-permute-done | bytes 1835040 | tf_op jit(solution)/shard_map/ppermute | solution.py:14
  74.6 17.9 %pad_maximum_fusion = bf16[256,36352]{0,1:T(8,128)(2,1)} fusion(bf16[256,32768]{0,1:T(8,128)(2,1)} %copy.22, bf16[256,3584]{0,1:T(8,128)(2,1)} %collective-permute-done), kind=kLoop, calls=%fused_computation.10 | loop fusion | flops 37224448 | bytes 37224448 | tf_op jit(solution)/shard_map/concatenate | solution.py:41
  92.6 52.4 %convert_bitcast_fusion = bf16[256,2,64,256]{0,3,1,2:T(8,128)(2,1)} fusion(bf16[256,71,512]{0,2,1:T(8,128)(2,1)} %bitcast.40, f32[512]{0:T(512)S(1)} %get-tuple-element.8, f32[512]{0:T(512)S(1)} %get-tuple-element.9, f32[512]{0:T(512)S(1)} %get-tuple-element.10, f32[512]{0:T(512)S(1)} %get-tuple-element.11, f32[512]{0:T(512)S(1)} %get-tuple-element.12, ...), kind=kOutput, calls=%fused_computation.14 | convolution fusion | flops 8800698368 | bytes 151535616 | tf_op jit(solution)/shard_map/kpn,isn->kpsi/dot_general | solution.py:50
  145.0 40.9 %copy.25 = bf16[256,2,64,256]{3,1,2,0:T(2,128)(2,1)} copy(bf16[256,2,64,256]{0,3,1,2:T(8,128)(2,1)} %convert_bitcast_fusion) | data formatting | bytes 33554432 | tf_op jit(solution)/shard_map/convert_element_type | solution.py:52
  185.8 368.7 %all_to_all.18 = bf16[256,2,64,256]{3,1,2,0:T(2,128)(2,1)S(1)} all-to-all(bf16[256,2,64,256]{3,1,2,0:T(2,128)(2,1)} %copy.25), channel_id=1, replica_groups=mesh['chan'=4,'row'=4,'col'=2] {'chan'}, dimensions={0} | all-to-all | bytes 33554432 | tf_op jit(solution)/shard_map/all_to_all | solution.py:53
  554.6 3.1 copy.26
  557.7 7.1 copy.38
  564.8 0.0 all-gather.2.cloned.1.call-update
  564.8 585.5 %all-gather.2.cloned.1.call-done = bf16[64,2,512,1024]{3,2,1,0:T(8,128)(2,1)} async-done(((bf16[64,2,64,1024]{3,2,1,0:T(8,128)(2,1)}), bf16[64,2,512,1024]{3,2,1,0:T(8,128)(2,1)}) %all-gather.2.cloned.1.call-update) | async-done | bytes 134217744 | tf_op jit(solution)/shard_map/all_gather | solution.py:62
  1150.3 23.8 %constant_dynamic-slice_fusion = (bf16[64,1,512,256]{3,2,1,0:T(8,128)(2,1)}, bf16[64,1,512,256]{3,2,1,0:T(8,128)(2,1)}) fusion(bf16[64,2,512,1024]{3,2,1,0:T(8,128)(2,1)} %all-gather.2.cloned.1.call-done, s32[]{:T(128)S(6)} %add.153, s32[]{:T(128)S(6)} %select_n.64), kind=kLoop, calls=%fused_computation.57 | loop fusion | flops 25165824 | bytes 67108872 | tf_op jit(solution)/shard_map/slice | solution.py:65
  1174.1 45.0 %fusion.15 = f32[64,1,256,512]{3,2,0,1:T(8,128)} fusion(bf16[64,2,512,1024]{3,2,1,0:T(8,128)(2,1)} %all-gather.2.cloned.1.call-done, s32[]{:T(128)S(6)} %select_n.65, s32[]{:T(128)S(6)} %select_n.64), kind=kOutput, calls=%fused_computation.16 | convolution fusion | flops 17179869184 | bytes 134217728 | tf_op jit(solution)/shard_map/cpsi,cpsj->cij/dot_general | solution.py:66
  1219.1 46.8 %fusion.10 = f32[64,1,256,512]{3,2,0,1:T(8,128)} fusion(bf16[64,2,512,1024]{3,2,1,0:T(8,128)(2,1)} %all-gather.2.cloned.1.call-done, s32[]{:T(128)S(6)} %select_n.65, bf16[64,1,512,256]{3,2,1,0:T(8,128)(2,1)} %get-tuple-element.6, bf16[64,1,512,256]{3,2,1,0:T(8,128)(2,1)} %get-tuple-element.5), kind=kOutput, calls=%fused_computation.15 | convolution fusion | flops 17196646400 | bytes 134217728 | tf_op jit(solution)/shard_map/cpsi,cpsj->cij/dot_general | solution.py:67
  1265.9 43.6 %maximum_multiply_fusion = f32[64,2,256,512]{3,2,0,1:T(8,128)} fusion(f32[64,1,256,512]{3,2,0,1:T(8,128)} %fusion.10, f32[64,1,256,512]{3,2,0,1:T(8,128)} %fusion.15), kind=kLoop, calls=%fused_computation | loop fusion | flops 33554432 | bytes 134217728 | tf_op jit(solution)/shard_map/div | solution.py:69
  1309.5 44.0 %copy.30 = f32[64,2,256,512]{3,2,1,0:T(8,128)} copy(f32[64,2,256,512]{3,2,0,1:T(8,128)} %maximum_multiply_fusion) | data formatting | bytes 134217728 | tf_op jit(solution)/shard_map/div | solution.py:69
  (1 shorter events, 0.0 us)
Async XLA Ops:
  6.5 1143.7 %all-gather.2.cloned.1.call-start = ((), (), s32[]{:S(2)}) async-start(), calls=%async_computation.1 | async-start | bytes 150994944 | tf_op jit(solution)/shard_map/all_gather | solution.py:62
  30.5 44.1 %collective-permute-start = (bf16[256,3584]{0,1:T(8,128)(2,1)S(1)}, bf16[256,3584]{0,1:T(8,128)(2,1)}, u32[]{:S(2)}, u32[]{:S(2)}) collective-permute-start(bf16[256,3584]{0,1:T(8,128)(2,1)S(1)} %slice.85), channel_id=1, source_target_pairs={{0,1},{1,2},{2,3},{3,4},{4,5},{5,6},{6,7},{8,9},{9,10},{10,11},{11... | collective-permute-start | bytes 5505032 | tf_op jit(solution)/shard_map/ppermute | solution.py:14
Sparse Core Ops, SparseCore 0:
  564.9 585.3 all-gather.1
where the time goes:
time: 1360 us
  waiting for transfers between devices  620 us (46%)
  blocking collectives  369 us (27%)
  matrix products  144 us (11%)
  local copies, waits for them, and re-layouts  119 us (9%)
  other arithmetic  88.3 us (6%)
  between operations  14.1 us (1%)
    all_gather x1, waiting for transfers between devices, per_device(): piece = lax.all_gather(turned, ('row', 'col'), axis=2, tiled=True)  585 us
    all_to_all x1, blocking collectives, per_device(): lax.all_to_all(spectra, 'chan', split_axis=0, concat_axis=3, tiled=True)  369 us
    dot_general x1, matrix products, per_device(): jnp.einsum('kpn,isn->kpsi', table, filtered, preferred_element_type=jnp.f...  52.4 us
    dot_general x1, matrix products, per_device(): jnp.einsum('cpsi,cpsj->cij', flipped, right, preferred_element_type=jnp.f...  46.8 us
    dot_general x1, matrix products, per_device(): jnp.einsum('cpsi,cpsj->cij', left, right, preferred_element_type=jnp.floa...  45 us
    div x1, local copies, waits for them, and re-layouts, per_device(): return summed / spectra_total  44 us
    div x1, other arithmetic, per_device(): return summed / spectra_total  43.6 us
    convert_element_type x1, local copies, waits for them, and re-layouts, per_device(): spectra = jnp.einsum('kpn,isn->kpsi', table, filtered, preferred_element_...  40.9 us
  transfers between devices with their start and end apart: 2, of which 2 were waited for; matrix products, arithmetic and copies ran while one was open for 0% of the time, Pallas kernels for 0%

commit v1 on v0

--- a/solution.py
+++ b/solution.py
@@ -1,11 +1,19 @@
+import functools
+
 import jax
 import jax.numpy as jnp
 from jax import lax
+from jax.experimental import pallas as pl
+from jax.experimental.pallas import tpu as pltpu
 from jax.sharding import PartitionSpec as P
 
 FFT_LEN = 512
 TAPS = 8
 CHANNELS = 256
+CHUNKS = 8
+STEP = 16
+ROWS = 32
+HALO = (TAPS - 1) * FFT_LEN
 
 
 def shifted(value, axis, by):
@@ -31,13 +39,153 @@
     return jnp.stack([jnp.cos(phase), -jnp.sin(phase)], axis=1).astype(jnp.bfloat16)
 
 
-def per_device(voltages):
+def filter_kernel(halo_ref, volt_ref, window_ref, table_ref, *rest):
+    outs, (ext, filt, turned) = rest[:-3], rest[-3:]
+    inputs = volt_ref.shape[0]
+    span = STEP * FFT_LEN
+
+    @pl.when(pl.program_id(0) == 0)
+    def _():
+        ext[:, :HALO] = halo_ref[...]
+
+    @pl.when(pl.program_id(0) > 0)
+    def _():
+        ext[:, :HALO] = ext[:, span : span + HALO]
+
+    ext[:, HALO:] = volt_ref[...]
+
+    @pl.loop(0, STEP)
+    def _(s):
+        for row in range(0, inputs, ROWS):
+            total = jnp.zeros((ROWS, FFT_LEN), jnp.float32)
+            for tap in range(TAPS):
+                start = pl.multiple_of((s + tap) * FFT_LEN, FFT_LEN)
+                block = ext[row : row + ROWS, pl.ds(start, FFT_LEN)]
+                total = total + window_ref[tap : tap + 1, :] * block.astype(jnp.float32)
+            filt[row : row + ROWS, :] = total.astype(jnp.bfloat16)
+        spectrum = lax.dot_general(
+            table_ref[...], filt[...], (((1,), (1,)), ((), ())), preferred_element_type=jnp.float32
+        )
+        for lane in range(inputs // 128):
+            turned[lane, pl.ds(s, spectrum.shape[0], stride=STEP), :] = spectrum[:, lane * 128 : (lane + 1) * 128]
+
+    count = turned.shape[1] // len(outs)
+    for chunk, out in enumerate(outs):
+        for lane in range(inputs // 128):
+            piece = turned[lane, chunk * count : (chunk + 1) * count, :].astype(jnp.bfloat16)
+            out[..., lane * 128 : (lane + 1) * 128] = piece.reshape(out.shape[:-1] + (128,))
+
+
+def filter_and_transform(halo, voltages, window, table, groups):
+    inputs, samples = voltages.shape
+    slots = samples // FFT_LEN
+    rows = table.shape[0]
+    width = CHANNELS // groups // CHUNKS
+    shape = (groups, width, 2, slots, inputs)
+    return pl.pallas_call(
+        filter_kernel,
+        grid=(slots // STEP,),
+        in_specs=[
+            pl.BlockSpec((inputs, HALO), lambda j: (0, 0)),
+            pl.BlockSpec((inputs, STEP * FFT_LEN), lambda j: (0, j)),
+            pl.BlockSpec((TAPS, FFT_LEN), lambda j: (0, 0)),
+            pl.BlockSpec((rows, FFT_LEN), lambda j: (0, 0)),
+        ],
+        out_specs=[pl.BlockSpec((groups, width, 2, STEP, inputs), lambda j: (0, 0, 0, j, 0))] * CHUNKS,
+        out_shape=[jax.ShapeDtypeStruct(shape, jnp.bfloat16)] * CHUNKS,
+        scratch_shapes=[
+            pltpu.VMEM((inputs, HALO + STEP * FFT_LEN), jnp.bfloat16),
+            pltpu.VMEM((inputs, FFT_LEN), jnp.bfloat16),
+            pltpu.VMEM((inputs // 128, rows * STEP, 128), jnp.float32),
+        ],
+        compiler_params=pltpu.CompilerParams(vmem_limit_bytes=50 * 2**20),
+        name="filter_and_transform",
+    )(halo, voltages, window, table)
+
+
+def tile_kernel(scale, place_ref, left_ref, right_ref, *rest):
+    out = rest[-1]
+    devices, _, _, parts, slots, inputs = left_ref.shape
+
+    def matrix(ref, index, part):
+        return ref[:, index, 0, part].reshape(devices * slots, inputs)
+
+    def product(left, right):
+        return lax.dot_general(left, right, (((0,), (0,)), ((), ())), preferred_element_type=jnp.float32)
+
+    for i in range(left_ref.shape[1]):
+        rows = slice(i * inputs, (i + 1) * inputs)
+        left = [matrix(left_ref, i, 0), matrix(left_ref, i, 1)]
+        for j in range(right_ref.shape[1]):
+            columns = slice(j * inputs, (j + 1) * inputs)
+            right = [matrix(right_ref, j, 0), matrix(right_ref, j, 1)]
+            out[0, 0, rows, columns] = (product(left[0], right[0]) + product(left[1], right[1])) * scale
+            out[0, 1, rows, columns] = (product(left[1], right[0]) - product(left[0], right[1])) * scale
+
+
+def tiles(piece, place, before, chunk, shape, scale):
+    devices, groups, width, parts, slots, inputs = piece.shape
+    rows, columns = shape[2] // inputs, shape[3] // inputs
+    in_specs = [
+        pl.BlockSpec((devices, rows, 1, parts, slots, inputs), lambda k, at: (0, at[0], k, 0, 0, 0)),
+        pl.BlockSpec((devices, columns, 1, parts, slots, inputs), lambda k, at: (0, at[1], k, 0, 0, 0)),
+    ]
+    operands = [place, piece, piece]
+    aliases = {}
+    if before is not None:
+        in_specs.append(pl.BlockSpec(memory_space=pl.ANY))
+        operands.append(before)
+        aliases = {3: 0}
+    moved = (rows + columns) * devices * width * parts * slots * inputs * 2
+    return pl.pallas_call(
+        functools.partial(tile_kernel, scale),
+        grid_spec=pltpu.PrefetchScalarGridSpec(
+            num_scalar_prefetch=1,
+            grid=(width,),
+            in_specs=in_specs,
+            out_specs=pl.BlockSpec((1,) + shape[1:], lambda k, at: (chunk * width + k, 0, 0, 0)),
+        ),
+        out_shape=jax.ShapeDtypeStruct(shape, jnp.float32),
+        input_output_aliases=aliases,
+        cost_estimate=pl.CostEstimate(
+            flops=8 * width * devices * slots * shape[2] * shape[3],
+            bytes_accessed=moved + width * 2 * shape[2] * shape[3] * 4,
+            transcendentals=0,
+        ),
+        compiler_params=pltpu.CompilerParams(vmem_limit_bytes=56 * 2**20),
+        name="visibility_tiles",
+    )(*operands)
+
+
+def chunked(voltages):
+    samples = voltages.shape[1]
+    groups = lax.axis_size("chan")
+    table = fourier_table(CHANNELS, FFT_LEN)
+    table = table.reshape(groups, CHUNKS, CHANNELS // groups // CHUNKS, 2, FFT_LEN)
+    table = table.transpose(1, 0, 2, 3, 4).reshape(2 * CHANNELS, FFT_LEN)
+    window = window_table(TAPS, FFT_LEN)
+    halo = shifted(voltages[:, samples - HALO :], ("row", "col"), 1)
+    chunks = filter_and_transform(halo, voltages, window, table, groups)
+    row_count = lax.axis_size("row")
+    col_count = lax.axis_size("col")
+    total_inputs = voltages.shape[0] * groups
+    spectra_total = samples // FFT_LEN * row_count * col_count
+    place = jnp.stack([lax.axis_index("row"), lax.axis_index("col")]).astype(jnp.int32)
+    shape = (CHANNELS // groups, 2, total_inputs // row_count, total_inputs // col_count)
+    out = None
+    for index, chunk in enumerate(chunks):
+        turned = lax.all_to_all(chunk, "chan", split_axis=0, concat_axis=0, tiled=True)
+        piece = lax.all_gather(turned, ("row", "col"), axis=0, tiled=False)
+        out = tiles(piece, place, out, index, shape, 1.0 / spectra_total)
+    return out
+
+
+def whole(voltages):
     local_inputs = voltages.shape[0]
     slot_spectra = voltages.shape[1] // FFT_LEN
     window = window_table(TAPS, FFT_LEN)
     table = fourier_table(CHANNELS, FFT_LEN)
-    tail = voltages[:, (slot_spectra - TAPS + 1) * FFT_LEN :]
-    earlier = shifted(tail, ("row", "col"), 1)
+    earlier = shifted(voltages[:, (slot_spectra - TAPS + 1) * FFT_LEN :], ("row", "col"), 1)
     extended = jnp.concatenate([earlier, voltages], axis=1).reshape(
         local_inputs, slot_spectra + TAPS - 1, FFT_LEN
     )
@@ -57,16 +205,23 @@
     row_block = inputs_all // row_count
     col_block = inputs_all // col_count
     spectra_total = slot_spectra * row_count * col_count
-    row_start = lax.axis_index("row") * row_block
-    col_start = lax.axis_index("col") * col_block
     piece = lax.all_gather(turned, ("row", "col"), axis=2, tiled=True)
-    left = lax.dynamic_slice_in_dim(piece, row_start, row_block, 3)
-    right = lax.dynamic_slice_in_dim(piece, col_start, col_block, 3)
+    left = lax.dynamic_slice_in_dim(piece, lax.axis_index("row") * row_block, row_block, 3)
+    right = lax.dynamic_slice_in_dim(piece, lax.axis_index("col") * col_block, col_block, 3)
     flipped = jnp.stack([left[:, 1], -left[:, 0]], axis=1)
     real_part = jnp.einsum("cpsi,cpsj->cij", left, right, preferred_element_type=jnp.float32)
     imag_part = jnp.einsum("cpsi,cpsj->cij", flipped, right, preferred_element_type=jnp.float32)
-    summed = jnp.stack([real_part, imag_part], axis=1)
-    return summed / spectra_total
+    return jnp.stack([real_part, imag_part], axis=1) / spectra_total
+
+
+def per_device(voltages):
+    inputs, samples = voltages.shape
+    groups = lax.axis_size("chan")
+    row_block = inputs * groups // lax.axis_size("row")
+    col_block = inputs * groups // lax.axis_size("col")
+    fits = inputs % 128 == 0 and row_block % inputs == 0 and col_block % inputs == 0
+    fits = fits and CHANNELS % (groups * CHUNKS) == 0 and samples % (STEP * FFT_LEN) == 0
+    return chunked(voltages) if fits else whole(voltages)
 
 
 def solution(mesh):

time: 1360 us -> 924 us (0.68)
  waiting for transfers between devices: 620 us -> 308 us
  Pallas kernels: 0 us -> 168 us
  matrix products: 144 us -> 0 us
  local copies, waits for them, and re-layouts: 119 us -> 15.1 us
  other arithmetic: 88.3 us -> 3.95 us
  blocking collectives: 369 us -> 407 us
    all_gather x1 -> x8, waiting for transfers between devices: 585 us -> 273 us  [chunked(): piece = lax.all_gather(turned, ('row', 'col'), axis=0, tiled=False)]
    pallas_call x0 -> x9, Pallas kernels: none -> 168 us  [the longest x8 104 us: tiles(): pl.pallas_call(functools.partial(tile_kernel, scale), grid_spec=pltpu.Pre...]
    dot_general x3 -> x0, matrix products: 144 us -> none  [the longest x1 52.4 us: per_device(): jnp.einsum('kpn,isn->kpsi', table, filtered, preferred_element_type=jnp.f...]
    div x1 -> x0, local copies, waits for them, and re-layouts: 44 us -> none  [per_device(): return summed / spectra_total]
    div x1 -> x0, other arithmetic: 43.6 us -> none  [per_device(): return summed / spectra_total]
    convert_element_type x1 -> x0, local copies, waits for them, and re-layouts: 40.9 us -> none  [per_device(): spectra = jnp.einsum('kpn,isn->kpsi', table, filtered, preferred_element_...]
    all_to_all x1 -> x8, blocking collectives: 369 us -> 407 us  [chunked(): lax.all_to_all(chunk, 'chan', split_axis=0, concat_axis=0, tiled=True)]
    slice x1 -> x0, other arithmetic: 23.8 us -> none  [per_device(): flipped = jnp.stack([left[:, 1], -left[:, 0]], axis=1)]
  transfers between devices with their start and end apart: 2 -> 9, of which waited for: 2 -> 5; matrix products, arithmetic and copies ran while one was open for 0% -> 1% of each run, Pallas kernels for 0% -> 10%
where the time goes in v1:
time: 924 us; the launch traced here: 922 us
  blocking collectives  407 us (44%)
  waiting for transfers between devices  308 us (33%)
  Pallas kernels  168 us (18%)
  local copies, waits for them, and re-layouts  15.1 us (2%)
  between operations  14.3 us (2%)
    all_to_all x8, blocking collectives, chunked(): lax.all_to_all(chunk, 'chan', split_axis=0, concat_axis=0, tiled=True)  407 us
    all_gather x8, waiting for transfers between devices, chunked(): piece = lax.all_gather(turned, ('row', 'col'), axis=0, tiled=False)  273 us
    pallas_call x8, Pallas kernels, tiles(): pl.pallas_call(functools.partial(tile_kernel, scale), grid_spec=pltpu.Pre...  104 us
    pallas_call x1, Pallas kernels, filter_and_transform(): pl.pallas_call(filter_kernel, grid=(slots // STEP,), in_specs=[pl.BlockSp...  64.6 us
    ppermute x1, waiting for transfers between devices, shifted(): return lax.ppermute(value, axis, pairs)  34.6 us
  transfers between devices with their start and end apart: 9, of which 5 were waited for; matrix products, arithmetic and copies ran while one was open for 1% of the time, Pallas kernels for 10%

profile of v1, /device:TPU:0, one launch (start us, length us, event | category | flops | bytes accessed | tf_op | source)
XLA Modules:
  0.0 922.2 jit_solution(16687556717354016398)
XLA Ops:
  6.5 0.0 all-gather.31.cloned.1.call-start
  6.5 2.8 slice.3
  9.4 4.9 collective-permute-start
  14.3 2.4 cosine_convert_fusion
  16.9 0.5 copy.9
  17.4 0.2 reshape.79.table_ref
  17.6 0.8 fusion.28
  19.1 0.1 fusion.34.window_ref
  19.2 34.6 %collective-permute-done.halo_ref = bf16[256,3584]{1,0:T(8,128)(2,1)S(1)} collective-permute-done((bf16[256,3584]{1,0:T(8,128)(2,1)}, bf16[256,3584]{1,0:T(8,128)(2,1)S(1)}, u32[]{:S(2)}, u32[]{:S(2)}) %collective-permute-start) | collective-permute-done | bytes 1835040 | tf_op jit(solution)/shard_map/ppermute | solution.py:22
  53.8 64.6 %filter_and_transform.1 = (bf16[4,8,2,64,256]{4,3,2,1,0:T(8,128)(2,1)}, bf16[4,8,2,64,256]{4,3,2,1,0:T(8,128)(2,1)}, bf16[4,8,2,64,256]{4,3,2,1,0:T(8,128)(2,1)}...) custom-call(bf16[256,3584]{1,0:T(8,128)(2,1)S(1)} %collective-permut, ...), custom_call_target="tpu_custom_call" | custom-call | tf_op jit(solution)/shard_map/filter_and_transform/pallas_call | solution.py:85
  118.4 53.8 %all_to_all.40 = bf16[4,8,2,64,256]{4,3,2,1,0:T(8,128)(2,1)} all-to-all(bf16[4,8,2,64,256]{4,3,2,1,0:T(8,128)(2,1)} %get-tuple-element.20), channel_id=1, replica_groups=mesh['chan'=4,'row'=4,'col'=2] {'chan'}, dimensions={0} | all-to-all | bytes 4194304 | tf_op jit(solution)/shard_map/all_to_all | solution.py:177
  172.1 0.0 copy-start.6
  172.1 0.0 all-gather.31.cloned.1.call-update
  172.2 0.0 all-gather.29.cloned.1.call-start
  172.2 1.5 copy-done.6
  173.7 51.2 %all_to_all.41 = bf16[4,8,2,64,256]{4,3,2,1,0:T(8,128)(2,1)} all-to-all(bf16[4,8,2,64,256]{4,3,2,1,0:T(8,128)(2,1)S(1)} %copy-done.6), channel_id=1, replica_groups=mesh['chan'=4,'row'=4,'col'=2] {'chan'}, dimensions={0} | all-to-all | bytes 4194304 | tf_op jit(solution)/shard_map/all_to_all | solution.py:177
  224.9 0.0 copy-start.5
  224.9 0.0 all-gather.29.cloned.1.call-update
  225.0 0.0 all-gather.27.cloned.1.call-start
  225.0 1.8 copy-done.5
  226.8 50.2 %all_to_all.42 = bf16[4,8,2,64,256]{4,3,2,1,0:T(8,128)(2,1)} all-to-all(bf16[4,8,2,64,256]{4,3,2,1,0:T(8,128)(2,1)S(1)} %copy-done.5), channel_id=1, replica_groups=mesh['chan'=4,'row'=4,'col'=2] {'chan'}, dimensions={0} | all-to-all | bytes 4194304 | tf_op jit(solution)/shard_map/all_to_all | solution.py:177
  277.0 0.0 copy-start.4
  277.0 0.0 all-gather.27.cloned.1.call-update
  277.1 0.0 all-gather.25.cloned.1.call-start
  277.1 1.5 copy-done.4
  278.6 50.4 %all_to_all.43 = bf16[4,8,2,64,256]{4,3,2,1,0:T(8,128)(2,1)} all-to-all(bf16[4,8,2,64,256]{4,3,2,1,0:T(8,128)(2,1)S(1)} %copy-done.4), channel_id=1, replica_groups=mesh['chan'=4,'row'=4,'col'=2] {'chan'}, dimensions={0} | all-to-all | bytes 4194304 | tf_op jit(solution)/shard_map/all_to_all | solution.py:177
  329.0 0.0 copy-start.3
  329.0 0.0 all-gather.25.cloned.1.call-update
  329.0 0.0 all-gather.23.cloned.1.call-start
  329.1 1.5 copy-done.3
  330.6 50.9 %all_to_all.44 = bf16[4,8,2,64,256]{4,3,2,1,0:T(8,128)(2,1)} all-to-all(bf16[4,8,2,64,256]{4,3,2,1,0:T(8,128)(2,1)S(1)} %copy-done.3), channel_id=1, replica_groups=mesh['chan'=4,'row'=4,'col'=2] {'chan'}, dimensions={0} | all-to-all | bytes 4194304 | tf_op jit(solution)/shard_map/all_to_all | solution.py:177
  381.5 0.0 copy-start.2
  381.5 0.0 all-gather.23.cloned.1.call-update
  381.5 0.0 all-gather.21.cloned.1.call-start
  381.5 1.5 copy-done.2
  383.1 50.5 %all_to_all.45 = bf16[4,8,2,64,256]{4,3,2,1,0:T(8,128)(2,1)} all-to-all(bf16[4,8,2,64,256]{4,3,2,1,0:T(8,128)(2,1)S(1)} %copy-done.2), channel_id=1, replica_groups=mesh['chan'=4,'row'=4,'col'=2] {'chan'}, dimensions={0} | all-to-all | bytes 4194304 | tf_op jit(solution)/shard_map/all_to_all | solution.py:177
  433.6 0.0 copy-start.1
  433.6 0.0 all-gather.21.cloned.1.call-update
  433.6 0.0 all-gather.19.cloned.1.call-start
  433.6 1.5 copy-done.1
  435.2 50.6 %all_to_all.46 = bf16[4,8,2,64,256]{4,3,2,1,0:T(8,128)(2,1)} all-to-all(bf16[4,8,2,64,256]{4,3,2,1,0:T(8,128)(2,1)S(1)} %copy-done.1), channel_id=1, replica_groups=mesh['chan'=4,'row'=4,'col'=2] {'chan'}, dimensions={0} | all-to-all | bytes 4194304 | tf_op jit(solution)/shard_map/all_to_all | solution.py:177
  485.7 0.0 copy-start
  485.7 0.0 all-gather.19.cloned.1.call-update
  485.8 0.0 all-gather.17.cloned.1.call-start
  485.8 2.1 copy-done
  488.0 49.9 %all_to_all.47 = bf16[4,8,2,64,256]{4,3,2,1,0:T(8,128)(2,1)} all-to-all(bf16[4,8,2,64,256]{4,3,2,1,0:T(8,128)(2,1)S(1)} %copy-done), channel_id=1, replica_groups=mesh['chan'=4,'row'=4,'col'=2] {'chan'}, dimensions={0} | all-to-all | bytes 4194304 | tf_op jit(solution)/shard_map/all_to_all | solution.py:177
  537.8 0.0 all-gather.17.cloned.1.call-update
  537.9 0.6 pad_add_fusion.place_ref
  538.4 0.0 all-gather.31.cloned.1.call-done
  538.4 13.5 %visibility_tiles.8.rest_0_ = f32[64,2,256,512]{3,2,1,0:T(8,128)} custom-call(s32[2]{0:T(128)} %pad_add_fusion.place_ref, bf16[8,4,8,2,64,256]{5,4,3,2,1,0:T(8,128)(2,1)} %bitcast.26, bf16[8,4,8,2,64,256]{5,4,3,2,1,0:T(8,128)(2,1)} %bitcast.27), custom_call_target="tpu_custom_call" | custom-call | flops 4294967296 | bytes 20971520 | tf_op jit(solution)/shard_map/visibility_tiles/pallas_call | solution.py:140
  551.9 0.0 all-gather.29.cloned.1.call-done
  551.9 12.7 %visibility_tiles.9.rest_0_ = f32[64,2,256,512]{3,2,1,0:T(8,128)} custom-call(s32[2]{0:T(128)} %pad_add_fusion.place_ref, bf16[8,4,8,2,64,256]{5,4,3,2,1,0:T(8,128)(2,1)} %bitcast.12, bf16[8,4,8,2,64,256]{5,4,3,2,1,0:T(8,128)(2,1)} %bitcast.13, f32[64,2,256,512]{3,2,1,0:T(8,128)} %visibility_tiles.8.rest_0_), custom_call_target="tpu_custom_call", output_to_operand_aliasing={{}: (3, {})} | custom-call | flops 4294967296 | bytes 20971520 | tf_op jit(solution)/shard_map/visibility_tiles/pallas_call | solution.py:140
  564.6 0.0 all-gather.27.cloned.1.call-done
  564.6 12.7 %visibility_tiles.10.rest_0_ = f32[64,2,256,512]{3,2,1,0:T(8,128)} custom-call(s32[2]{0:T(128)} %pad_add_fusion.place_ref, bf16[8,4,8,2,64,256]{5,4,3,2,1,0:T(8,128)(2,1)} %bitcast.14, bf16[8,4,8,2,64,256]{5,4,3,2,1,0:T(8,128)(2,1)} %bitcast.15, f32[64,2,256,512]{3,2,1,0:T(8,128)} %visibility_tiles.9.rest_0_), custom_call_target="tpu_custom_call", output_to_operand_aliasing={{}: (3, {})} | custom-call | flops 4294967296 | bytes 20971520 | tf_op jit(solution)/shard_map/visibility_tiles/pallas_call | solution.py:140
  577.3 0.0 all-gather.25.cloned.1.call-done
  577.3 13.1 %visibility_tiles.11.rest_0_ = f32[64,2,256,512]{3,2,1,0:T(8,128)} custom-call(s32[2]{0:T(128)} %pad_add_fusion.place_ref, bf16[8,4,8,2,64,256]{5,4,3,2,1,0:T(8,128)(2,1)} %bitcast.16, bf16[8,4,8,2,64,256]{5,4,3,2,1,0:T(8,128)(2,1)} %bitcast.17, f32[64,2,256,512]{3,2,1,0:T(8,128)} %visibility_tiles.10.rest_0_), custom_call_target="tpu_custom_call", output_to_operand_aliasing={{}: (3, {})} | custom-call | flops 4294967296 | bytes 20971520 | tf_op jit(solution)/shard_map/visibility_tiles/pallas_call | solution.py:140
  590.4 37.2 %all-gather.23.cloned.1.call-done = bf16[32,8,2,64,256]{4,3,2,1,0:T(8,128)(2,1)} async-done(((bf16[4,8,2,64,256]{4,3,2,1,0:T(8,128)(2,1)}), bf16[32,8,2,64,256]{4,3,2,1,0:T(8,128)(2,1)}) %all-gather.23.cloned.1.call-update) | async-done | bytes 16777232 | tf_op jit(solution)/shard_map/all_gather | solution.py:178
  627.6 13.1 %visibility_tiles.12.rest_0_ = f32[64,2,256,512]{3,2,1,0:T(8,128)} custom-call(s32[2]{0:T(128)} %pad_add_fusion.place_ref, bf16[8,4,8,2,64,256]{5,4,3,2,1,0:T(8,128)(2,1)} %bitcast.18, bf16[8,4,8,2,64,256]{5,4,3,2,1,0:T(8,128)(2,1)} %bitcast.19, f32[64,2,256,512]{3,2,1,0:T(8,128)} %visibility_tiles.11.rest_0_), custom_call_target="tpu_custom_call", output_to_operand_aliasing={{}: (3, {})} | custom-call | flops 4294967296 | bytes 20971520 | tf_op jit(solution)/shard_map/visibility_tiles/pallas_call | solution.py:140
  640.7 78.5 %all-gather.21.cloned.1.call-done = bf16[32,8,2,64,256]{4,3,2,1,0:T(8,128)(2,1)} async-done(((bf16[4,8,2,64,256]{4,3,2,1,0:T(8,128)(2,1)}), bf16[32,8,2,64,256]{4,3,2,1,0:T(8,128)(2,1)}) %all-gather.21.cloned.1.call-update) | async-done | bytes 16777232 | tf_op jit(solution)/shard_map/all_gather | solution.py:178
  719.2 13.1 %visibility_tiles.13.rest_0_ = f32[64,2,256,512]{3,2,1,0:T(8,128)} custom-call(s32[2]{0:T(128)} %pad_add_fusion.place_ref, bf16[8,4,8,2,64,256]{5,4,3,2,1,0:T(8,128)(2,1)} %bitcast.20, bf16[8,4,8,2,64,256]{5,4,3,2,1,0:T(8,128)(2,1)} %bitcast.21, f32[64,2,256,512]{3,2,1,0:T(8,128)} %visibility_tiles.12.rest_0_), custom_call_target="tpu_custom_call", output_to_operand_aliasing={{}: (3, {})} | custom-call | flops 4294967296 | bytes 20971520 | tf_op jit(solution)/shard_map/visibility_tiles/pallas_call | solution.py:140
  732.3 78.7 %all-gather.19.cloned.1.call-done = bf16[32,8,2,64,256]{4,3,2,1,0:T(8,128)(2,1)} async-done(((bf16[4,8,2,64,256]{4,3,2,1,0:T(8,128)(2,1)}), bf16[32,8,2,64,256]{4,3,2,1,0:T(8,128)(2,1)}) %all-gather.19.cloned.1.call-update) | async-done | bytes 16777232 | tf_op jit(solution)/shard_map/all_gather | solution.py:178
  810.9 13.1 %visibility_tiles.14.rest_0_ = f32[64,2,256,512]{3,2,1,0:T(8,128)} custom-call(s32[2]{0:T(128)} %pad_add_fusion.place_ref, bf16[8,4,8,2,64,256]{5,4,3,2,1,0:T(8,128)(2,1)} %bitcast.22, bf16[8,4,8,2,64,256]{5,4,3,2,1,0:T(8,128)(2,1)} %bitcast.23, f32[64,2,256,512]{3,2,1,0:T(8,128)} %visibility_tiles.13.rest_0_), custom_call_target="tpu_custom_call", output_to_operand_aliasing={{}: (3, {})} | custom-call | flops 4294967296 | bytes 20971520 | tf_op jit(solution)/shard_map/visibility_tiles/pallas_call | solution.py:140
  824.0 78.7 %all-gather.17.cloned.1.call-done = bf16[32,8,2,64,256]{4,3,2,1,0:T(8,128)(2,1)} async-done(((bf16[4,8,2,64,256]{4,3,2,1,0:T(8,128)(2,1)}), bf16[32,8,2,64,256]{4,3,2,1,0:T(8,128)(2,1)}) %all-gather.17.cloned.1.call-update) | async-done | bytes 16777232 | tf_op jit(solution)/shard_map/all_gather | solution.py:178
  902.7 12.7 %visibility_tiles.15 = f32[64,2,256,512]{3,2,1,0:T(8,128)} custom-call(s32[2]{0:T(128)} %pad_add_fusion.place_ref, bf16[8,4,8,2,64,256]{5,4,3,2,1,0:T(8,128)(2,1)} %bitcast.24, bf16[8,4,8,2,64,256]{5,4,3,2,1,0:T(8,128)(2,1)} %bitcast.25, f32[64,2,256,512]{3,2,1,0:T(8,128)} %visibility_tiles.14.rest_0_), custom_call_target="tpu_custom_call", output_to_operand_aliasing={{}: (3, {})} | custom-call | flops 4294967296 | bytes 20971520 | tf_op jit(solution)/shard_map/visibility_tiles/pallas_call | solution.py:140
  (2 shorter events, 0.1 us)
Async XLA Ops:
  6.5 531.9 %all-gather.31.cloned.1.call-start = ((), (), s32[]{:S(2)}) async-start(), calls=%async_computation.15 | async-start | bytes 18874368 | tf_op jit(solution)/shard_map/all_gather | solution.py:178
  9.4 44.4 %collective-permute-start = (bf16[256,3584]{1,0:T(8,128)(2,1)}, bf16[256,3584]{1,0:T(8,128)(2,1)S(1)}, u32[]{:S(2)}, u32[]{:S(2)}) collective-permute-start(bf16[256,3584]{1,0:T(8,128)(2,1)} %slice.3), channel_id=1, source_target_pairs={{0,1},{1,2},{2,3},{3,4},{4,5},{5,6},{6,7},{8,9},{9,10},{10,11},{11... | collective-permute-start | bytes 5505032 | tf_op jit(solution)/shard_map/ppermute | solution.py:22
  172.1 1.6 copy-start.6
  172.2 379.8 %all-gather.29.cloned.1.call-start = ((), (), s32[]{:S(2)}) async-start(), calls=%async_computation.14 | async-start | bytes 18874368 | tf_op jit(solution)/shard_map/all_gather | solution.py:178
  224.9 1.9 copy-start.5
  225.0 339.6 %all-gather.27.cloned.1.call-start = ((), (), s32[]{:S(2)}) async-start(), calls=%async_computation.13 | async-start | bytes 18874368 | tf_op jit(solution)/shard_map/all_gather | solution.py:178
  277.0 1.6 copy-start.4
  277.1 300.2 %all-gather.25.cloned.1.call-start = ((), (), s32[]{:S(2)}) async-start(), calls=%async_computation.12 | async-start | bytes 18874368 | tf_op jit(solution)/shard_map/all_gather | solution.py:178
  329.0 1.6 copy-start.3
  329.0 298.5 %all-gather.23.cloned.1.call-start = ((), (), s32[]{:S(2)}) async-start(), calls=%async_computation.11 | async-start | bytes 18874368 | tf_op jit(solution)/shard_map/all_gather | solution.py:178
  381.5 1.6 copy-start.2
  381.5 337.7 %all-gather.21.cloned.1.call-start = ((), (), s32[]{:S(2)}) async-start(), calls=%async_computation.10 | async-start | bytes 18874368 | tf_op jit(solution)/shard_map/all_gather | solution.py:178
  433.6 1.6 copy-start.1
  433.6 377.3 %all-gather.19.cloned.1.call-start = ((), (), s32[]{:S(2)}) async-start(), calls=%async_computation.9 | async-start | bytes 18874368 | tf_op jit(solution)/shard_map/all_gather | solution.py:178
  485.7 2.2 copy-start
  485.8 416.9 %all-gather.17.cloned.1.call-start = ((), (), s32[]{:S(2)}) async-start(), calls=%async_computation.8 | async-start | bytes 18874368 | tf_op jit(solution)/shard_map/all_gather | solution.py:178
Sparse Core Ops, SparseCore 0:
  172.3 88.3 all-gather.30
  262.6 89.8 all-gather.28
  354.4 89.8 all-gather.26
  446.0 89.8 all-gather.24
  537.6 89.9 all-gather.22
  629.3 89.8 all-gather.20
  721.0 89.8 all-gather.18
  812.8 89.8 all-gather.16

commit v2 on v1

--- a/solution.py
+++ b/solution.py
@@ -10,7 +10,8 @@
 FFT_LEN = 512
 TAPS = 8
 CHANNELS = 256
-CHUNKS = 8
+PARTS = (1, 2, 3, 2)
+EIGHTHS = sum(PARTS)
 STEP = 16
 ROWS = 32
 HALO = (TAPS - 1) * FFT_LEN
@@ -40,7 +41,7 @@
 
 
 def filter_kernel(halo_ref, volt_ref, window_ref, table_ref, *rest):
-    outs, (ext, filt, turned) = rest[:-3], rest[-3:]
+    outs, (ext, filt, turned) = rest[-3 - len(PARTS) : -3], rest[-3:]
     inputs = volt_ref.shape[0]
     span = STEP * FFT_LEN
 
@@ -69,30 +70,39 @@
         for lane in range(inputs // 128):
             turned[lane, pl.ds(s, spectrum.shape[0], stride=STEP), :] = spectrum[:, lane * 128 : (lane + 1) * 128]
 
-    count = turned.shape[1] // len(outs)
+    unit = turned.shape[1] // EIGHTHS
     for chunk, out in enumerate(outs):
+        first, last = sum(PARTS[:chunk]) * unit, sum(PARTS[: chunk + 1]) * unit
         for lane in range(inputs // 128):
-            piece = turned[lane, chunk * count : (chunk + 1) * count, :].astype(jnp.bfloat16)
+            piece = turned[lane, first:last, :].astype(jnp.bfloat16)
             out[..., lane * 128 : (lane + 1) * 128] = piece.reshape(out.shape[:-1] + (128,))
 
 
-def filter_and_transform(halo, voltages, window, table, groups):
+def filter_and_transform(halo, voltages, window, table, groups, first, steps, before=()):
     inputs, samples = voltages.shape
     slots = samples // FFT_LEN
     rows = table.shape[0]
-    width = CHANNELS // groups // CHUNKS
-    shape = (groups, width, 2, slots, inputs)
+    widths = [part * CHANNELS // groups // EIGHTHS for part in PARTS]
     return pl.pallas_call(
         filter_kernel,
-        grid=(slots // STEP,),
+        grid=(steps,),
         in_specs=[
             pl.BlockSpec((inputs, HALO), lambda j: (0, 0)),
-            pl.BlockSpec((inputs, STEP * FFT_LEN), lambda j: (0, j)),
+            pl.BlockSpec((inputs, STEP * FFT_LEN), lambda j: (0, j + first)),
             pl.BlockSpec((TAPS, FFT_LEN), lambda j: (0, 0)),
             pl.BlockSpec((rows, FFT_LEN), lambda j: (0, 0)),
+        ]
+        + [pl.BlockSpec(memory_space=pl.ANY)] * len(before),
+        out_specs=[
+            pl.BlockSpec((groups, width, 2, STEP, inputs), lambda j: (0, 0, 0, j + first, 0)) for width in widths
         ],
-        out_specs=[pl.BlockSpec((groups, width, 2, STEP, inputs), lambda j: (0, 0, 0, j, 0))] * CHUNKS,
-        out_shape=[jax.ShapeDtypeStruct(shape, jnp.bfloat16)] * CHUNKS,
+        out_shape=[jax.ShapeDtypeStruct((groups, width, 2, slots, inputs), jnp.bfloat16) for width in widths],
+        input_output_aliases={4 + chunk: chunk for chunk in range(len(before))},
+        cost_estimate=pl.CostEstimate(
+            flops=2 * rows * FFT_LEN * inputs * steps * STEP * 4,
+            bytes_accessed=4 * steps * STEP * FFT_LEN * inputs,
+            transcendentals=0,
+        ),
         scratch_shapes=[
             pltpu.VMEM((inputs, HALO + STEP * FFT_LEN), jnp.bfloat16),
             pltpu.VMEM((inputs, FFT_LEN), jnp.bfloat16),
@@ -100,7 +110,7 @@
         ],
         compiler_params=pltpu.CompilerParams(vmem_limit_bytes=50 * 2**20),
         name="filter_and_transform",
-    )(halo, voltages, window, table)
+    )(halo, voltages, window, table, *before)
 
 
 def tile_kernel(scale, place_ref, left_ref, right_ref, *rest):
@@ -123,7 +133,7 @@
             out[0, 1, rows, columns] = (product(left[1], right[0]) - product(left[0], right[1])) * scale
 
 
-def tiles(piece, place, before, chunk, shape, scale):
+def tiles(piece, place, before, start, shape, scale):
     devices, groups, width, parts, slots, inputs = piece.shape
     rows, columns = shape[2] // inputs, shape[3] // inputs
     in_specs = [
@@ -143,7 +153,7 @@
             num_scalar_prefetch=1,
             grid=(width,),
             in_specs=in_specs,
-            out_specs=pl.BlockSpec((1,) + shape[1:], lambda k, at: (chunk * width + k, 0, 0, 0)),
+            out_specs=pl.BlockSpec((1,) + shape[1:], lambda k, at: (start + k, 0, 0, 0)),
         ),
         out_shape=jax.ShapeDtypeStruct(shape, jnp.float32),
         input_output_aliases=aliases,
@@ -161,22 +171,28 @@
     samples = voltages.shape[1]
     groups = lax.axis_size("chan")
     table = fourier_table(CHANNELS, FFT_LEN)
-    table = table.reshape(groups, CHUNKS, CHANNELS // groups // CHUNKS, 2, FFT_LEN)
-    table = table.transpose(1, 0, 2, 3, 4).reshape(2 * CHANNELS, FFT_LEN)
+    table = table.reshape(groups, EIGHTHS, CHANNELS // groups // EIGHTHS, 2, FFT_LEN)
+    ends = [sum(PARTS[: chunk + 1]) for chunk in range(len(PARTS))]
+    table = [table[:, end - part : end].reshape(-1, FFT_LEN) for end, part in zip(ends, PARTS)]
+    table = jnp.concatenate(table, axis=0)
     window = window_table(TAPS, FFT_LEN)
     halo = shifted(voltages[:, samples - HALO :], ("row", "col"), 1)
-    chunks = filter_and_transform(halo, voltages, window, table, groups)
+    steps = samples // (STEP * FFT_LEN)
+    own = voltages[:, STEP * FFT_LEN - HALO : STEP * FFT_LEN]
+    chunks = filter_and_transform(own, voltages, window, table, groups, 1, steps - 1)
+    chunks = filter_and_transform(halo, voltages, window, table, groups, 0, 1, chunks)
     row_count = lax.axis_size("row")
     col_count = lax.axis_size("col")
     total_inputs = voltages.shape[0] * groups
     spectra_total = samples // FFT_LEN * row_count * col_count
     place = jnp.stack([lax.axis_index("row"), lax.axis_index("col")]).astype(jnp.int32)
     shape = (CHANNELS // groups, 2, total_inputs // row_count, total_inputs // col_count)
-    out = None
-    for index, chunk in enumerate(chunks):
+    out, start = None, 0
+    for chunk in chunks:
         turned = lax.all_to_all(chunk, "chan", split_axis=0, concat_axis=0, tiled=True)
         piece = lax.all_gather(turned, ("row", "col"), axis=0, tiled=False)
-        out = tiles(piece, place, out, index, shape, 1.0 / spectra_total)
+        out = tiles(piece, place, out, start, shape, 1.0 / spectra_total)
+        start += chunk.shape[1]
     return out
 
 
@@ -220,7 +236,8 @@
     row_block = inputs * groups // lax.axis_size("row")
     col_block = inputs * groups // lax.axis_size("col")
     fits = inputs % 128 == 0 and row_block % inputs == 0 and col_block % inputs == 0
-    fits = fits and CHANNELS % (groups * CHUNKS) == 0 and samples % (STEP * FFT_LEN) == 0
+    fits = fits and CHANNELS % (groups * EIGHTHS) == 0 and samples % (STEP * FFT_LEN) == 0
+    fits = fits and samples > STEP * FFT_LEN
     return chunked(voltages) if fits else whole(voltages)
 
 

time: 924 us -> 829 us (0.90)
  waiting for transfers between devices: 308 us -> 242 us
  blocking collectives: 407 us -> 391 us
  local copies, waits for them, and re-layouts: 15.1 us -> 4.24 us
    ppermute x1, waiting for transfers between devices: 34.6 us -> 0.01 us  [shifted(): return lax.ppermute(value, axis, pairs)]
    all_gather x8 -> x4, waiting for transfers between devices: 273 us -> 242 us  [chunked(): piece = lax.all_gather(turned, ('row', 'col'), axis=0, tiled=False)]
    all_to_all x8 -> x4, blocking collectives: 407 us -> 391 us  [chunked(): lax.all_to_all(chunk, 'chan', split_axis=0, concat_axis=0, tiled=True)]
    unnamed x14 -> x3, local copies, waits for them, and re-layouts: 11.5 us -> 0.03 us
    pallas_call x8 -> x4, Pallas kernels: 104 us -> 96.1 us  [tiles(): pl.pallas_call(functools.partial(tile_kernel, scale), grid_spec=pltpu.Pre...]
    pallas_call x1 -> x2, Pallas kernels: 64.6 us -> 69.3 us  [filter_and_transform(): pl.pallas_call(filter_kernel, grid=(steps,), in_specs=[pl.BlockSpec((inpu...]
  transfers between devices with their start and end apart: 9 -> 5, of which waited for: 5 -> 2; matrix products, arithmetic and copies ran while one was open for 1% -> 1% of each run, Pallas kernels for 10% -> 15%
where the time goes in v2:
time: 829 us; the launch traced here: 827 us
  blocking collectives  391 us (47%)
  waiting for transfers between devices  242 us (29%)
  Pallas kernels  165 us (20%)
  between operations  13.9 us (2%)
    all_to_all x4, blocking collectives, chunked(): lax.all_to_all(chunk, 'chan', split_axis=0, concat_axis=0, tiled=True)  391 us
    all_gather x4, waiting for transfers between devices, chunked(): piece = lax.all_gather(turned, ('row', 'col'), axis=0, tiled=False)  242 us
    pallas_call x4, Pallas kernels, tiles(): pl.pallas_call(functools.partial(tile_kernel, scale), grid_spec=pltpu.Pre...  96.1 us
    pallas_call x2, Pallas kernels, filter_and_transform(): pl.pallas_call(filter_kernel, grid=(steps,), in_specs=[pl.BlockSpec((inpu...  69.3 us
  transfers between devices with their start and end apart: 5, of which 2 were waited for; matrix products, arithmetic and copies ran while one was open for 1% of the time, Pallas kernels for 15%

profile of v2, /device:TPU:0, one launch (start us, length us, event | category | flops | bytes accessed | tf_op | source)
XLA Modules:
  0.0 826.9 jit_solution(17978375957458097153)
XLA Ops:
  6.5 0.0 all-gather.15.cloned.1.call-start
  6.5 3.5 fusion.35
  10.1 6.1 collective-permute-start
  16.2 2.4 cosine_convert_fusion
  18.7 0.7 fusion.28
  19.4 0.1 copy.10
  19.5 0.1 reshape.89
  19.6 0.1 copy.9
  19.7 0.2 copy.11
  19.9 0.1 reshape.90
  20.0 0.1 copy.12
  20.1 0.1 reshape.91
  20.8 0.1 fusion.34.window_ref
  21.0 49.4 %filter_and_transform.2 = (bf16[4,8,2,64,256]{4,3,2,1,0:T(8,128)(2,1)}, bf16[4,16,2,64,256]{4,3,2,1,0:T(8,128)(2,1)}, bf16[4,24,2,64,256]{4,3,2,1,0:T(8,128)(2,1)}, bf16[4,16,2,64,256]{4,3,2,1,0:T(8,128)(2,1)}) custom-call(bf16[256,3584]{1,0:T(8,128)(2,1)S(1)} %get-tuple-element.21.halo_ref, bf16[256,32768]{1,0:T(8,128)(2,1)} %volt_ref.3, ...), custom_call_target="tpu_custom_call" | custom-call | flops 25769803776 | bytes 25165824 | tf_op jit(solution)/shard_map/filter_and_transform/pallas_call | solution.py:86
  70.4 0.0 collective-permute-done.halo_ref
  70.4 19.8 %filter_and_transform.3 = (bf16[4,8,2,64,256]{4,3,2,1,0:T(8,128)(2,1)}, bf16[4,16,2,64,256]{4,3,2,1,0:T(8,128)(2,1)}, bf16[4,24,2,64,256]{4,3,2,1,0:T(8,128)(2,1)}, bf16[4,16,2,64,256]{4,3,2,1,0:T(8,128)(2,1)}) custom-call(bf16[256,3584]{1,0:T(8,128)(2,1)} %collective-permute-done.halo_ref, ...), custom_call_target="tpu_custom_call", output_to_operand_aliasing={{0}: (4, {}), {1}: (5, {}), {2}: (6, {}), {3}: (7, {})} | custom-call | flops 8589934592 | bytes 8388608 | tf_op jit(solution)/shard_map/filter_and_transform/pallas_call | solution.py:86
  90.2 51.7 %all_to_all.20 = bf16[4,8,2,64,256]{4,3,2,1,0:T(8,128)(2,1)} all-to-all(bf16[4,8,2,64,256]{4,3,2,1,0:T(8,128)(2,1)} %get-tuple-element.20), channel_id=1, replica_groups=mesh['chan'=4,'row'=4,'col'=2] {'chan'}, dimensions={0} | all-to-all | bytes 4194304 | tf_op jit(solution)/shard_map/all_to_all | solution.py:192
  141.9 0.0 all-gather.15.cloned.1.call-update
  141.9 0.0 all-gather.13.cloned.1.call-start
  142.0 97.7 %all_to_all.21 = bf16[4,16,2,64,256]{4,3,2,1,0:T(8,128)(2,1)} all-to-all(bf16[4,16,2,64,256]{4,3,2,1,0:T(8,128)(2,1)} %get-tuple-element.19), channel_id=1, replica_groups=mesh['chan'=4,'row'=4,'col'=2] {'chan'}, dimensions={0} | all-to-all | bytes 8388608 | tf_op jit(solution)/shard_map/all_to_all | solution.py:192
  239.7 0.0 all-gather.13.cloned.1.call-update
  239.7 0.0 all-gather.11.cloned.1.call-start
  239.8 143.8 %all_to_all.22 = bf16[4,24,2,64,256]{4,3,2,1,0:T(8,128)(2,1)} all-to-all(bf16[4,24,2,64,256]{4,3,2,1,0:T(8,128)(2,1)} %get-tuple-element.18), channel_id=1, replica_groups=mesh['chan'=4,'row'=4,'col'=2] {'chan'}, dimensions={0} | all-to-all | bytes 12582912 | tf_op jit(solution)/shard_map/all_to_all | solution.py:192
  383.6 0.0 all-gather.11.cloned.1.call-update
  383.6 0.0 all-gather.9.cloned.1.call-start
  383.7 98.0 %all_to_all.23 = bf16[4,16,2,64,256]{4,3,2,1,0:T(8,128)(2,1)} all-to-all(bf16[4,16,2,64,256]{4,3,2,1,0:T(8,128)(2,1)} %get-tuple-element.17), channel_id=1, replica_groups=mesh['chan'=4,'row'=4,'col'=2] {'chan'}, dimensions={0} | all-to-all | bytes 8388608 | tf_op jit(solution)/shard_map/all_to_all | solution.py:192
  481.6 0.0 all-gather.9.cloned.1.call-update
  481.7 0.6 pad_add_fusion.place_ref
  482.3 0.0 all-gather.15.cloned.1.call-done
  482.3 12.8 %visibility_tiles.4.rest_0_ = f32[64,2,256,512]{3,2,1,0:T(8,128)} custom-call(s32[2]{0:T(128)} %pad_add_fusion.place_ref, bf16[8,4,8,2,64,256]{5,4,3,2,1,0:T(8,128)(2,1)} %bitcast.14, bf16[8,4,8,2,64,256]{5,4,3,2,1,0:T(8,128)(2,1)} %bitcast.15), custom_call_target="tpu_custom_call" | custom-call | flops 4294967296 | bytes 20971520 | tf_op jit(solution)/shard_map/visibility_tiles/pallas_call | solution.py:150
  495.1 0.0 all-gather.13.cloned.1.call-done
  495.1 24.8 %visibility_tiles.5.rest_0_ = f32[64,2,256,512]{3,2,1,0:T(8,128)} custom-call(s32[2]{0:T(128)} %pad_add_fusion.place_ref, bf16[8,4,16,2,64,256]{5,4,3,2,1,0:T(8,128)(2,1)} %bitcast.10, bf16[8,4,16,2,64,256]{5,4,3,2,1,0:T(8,128)(2,1)} %bitcast.11, f32[64,2,256,512]{3,2,1,0:T(8,128)} %visibility_tiles.4.rest_0_), custom_call_target="tpu_custom_call", output_to_operand_aliasing={{}: (3, {})} | custom-call | flops 8589934592 | bytes 41943040 | tf_op jit(solution)/shard_map/visibility_tiles/pallas_call | solution.py:150
  519.9 114.6 %all-gather.11.cloned.1.call-done = bf16[32,24,2,64,256]{4,3,2,1,0:T(8,128)(2,1)} async-done(((bf16[4,24,2,64,256]{4,3,2,1,0:T(8,128)(2,1)}), bf16[32,24,2,64,256]{4,3,2,1,0:T(8,128)(2,1)}) %all-gather.11.cloned.1.call-update) | async-done | bytes 50331664 | tf_op jit(solution)/shard_map/all_gather | solution.py:193
  634.6 35.2 %visibility_tiles.6.rest_0_ = f32[64,2,256,512]{3,2,1,0:T(8,128)} custom-call(s32[2]{0:T(128)} %pad_add_fusion.place_ref, bf16[8,4,24,2,64,256]{5,4,3,2,1,0:T(8,128)(2,1)} %bitcast.8, bf16[8,4,24,2,64,256]{5,4,3,2,1,0:T(8,128)(2,1)} %bitcast.9, f32[64,2,256,512]{3,2,1,0:T(8,128)} %visibility_tiles.5.rest_0_), custom_call_target="tpu_custom_call", output_to_operand_aliasing={{}: (3, {})} | custom-call | flops 12884901888 | bytes 62914560 | tf_op jit(solution)/shard_map/visibility_tiles/pallas_call | solution.py:150
  669.7 127.4 %all-gather.9.cloned.1.call-done = bf16[32,16,2,64,256]{4,3,2,1,0:T(8,128)(2,1)} async-done(((bf16[4,16,2,64,256]{4,3,2,1,0:T(8,128)(2,1)}), bf16[32,16,2,64,256]{4,3,2,1,0:T(8,128)(2,1)}) %all-gather.9.cloned.1.call-update) | async-done | bytes 33554448 | tf_op jit(solution)/shard_map/all_gather | solution.py:193
  797.1 23.2 %visibility_tiles.7 = f32[64,2,256,512]{3,2,1,0:T(8,128)} custom-call(s32[2]{0:T(128)} %pad_add_fusion.place_ref, bf16[8,4,16,2,64,256]{5,4,3,2,1,0:T(8,128)(2,1)} %bitcast.12, bf16[8,4,16,2,64,256]{5,4,3,2,1,0:T(8,128)(2,1)} %bitcast.13, f32[64,2,256,512]{3,2,1,0:T(8,128)} %visibility_tiles.6.rest_0_), custom_call_target="tpu_custom_call", output_to_operand_aliasing={{}: (3, {})} | custom-call | flops 8589934592 | bytes 41943040 | tf_op jit(solution)/shard_map/visibility_tiles/pallas_call | solution.py:150
  (9 shorter events, 0.1 us)
Async XLA Ops:
  6.5 475.7 %all-gather.15.cloned.1.call-start = ((), (), s32[]{:S(2)}) async-start(), calls=%async_computation.7 | async-start | bytes 18874368 | tf_op jit(solution)/shard_map/all_gather | solution.py:193
  10.1 60.4 %collective-permute-start = (bf16[256,3584]{1,0:T(8,128)(2,1)}, bf16[256,3584]{1,0:T(8,128)(2,1)}, u32[]{:S(2)}, u32[]{:S(2)}) collective-permute-start(bf16[256,3584]{1,0:T(8,128)(2,1)} %get-tuple-element.22), channel_id=1, source_target_pairs={{0,1},{1,2},{2,3},{3,4},{4,5},{5,6},{6,7},{8,9},{9,10},{10,11},{11... | collective-permute-start | bytes 5505032 | tf_op jit(solution)/shard_map/ppermute | solution.py:23
  141.9 353.2 %all-gather.13.cloned.1.call-start = ((), (), s32[]{:S(2)}) async-start(), calls=%async_computation.6 | async-start | bytes 37748736 | tf_op jit(solution)/shard_map/all_gather | solution.py:193
  239.7 394.9 %all-gather.11.cloned.1.call-start = ((), (), s32[]{:S(2)}) async-start(), calls=%async_computation.5 | async-start | bytes 56623104 | tf_op jit(solution)/shard_map/all_gather | solution.py:193
  383.6 413.5 %all-gather.9.cloned.1.call-start = ((), (), s32[]{:S(2)}) async-start(), calls=%async_computation.4 | async-start | bytes 37748736 | tf_op jit(solution)/shard_map/all_gather | solution.py:193
Sparse Core Ops, SparseCore 0:
  142.0 88.0 all-gather.14
  239.8 160.5 all-gather.12
  402.3 232.1 all-gather.10
  636.3 160.7 all-gather.8
